TPU v7x, 128 devices: a whole 4x4x4 slice. The times are simulated.
128 devices in a mesh: dp: 128 (over y, x, z, core).
Axes of the slice: x: 4, y: 4, z: 4, core: 2. Of those that a mesh axis runs over, the one named last changes fastest.
Arguments:
- tokens: bfloat16 [73728, 2048], P('dp'), may hold values from -24 to 24
- route_gate: bfloat16 [73728], P('dp'), may hold values from 0.049804688 to 1
- cotangent: bfloat16 [73728, 2048], P('dp'), may hold values from -6 to 6
- row_count: int32 [128], P('dp'), may hold values from 1 to 576, 24576 in all
- w_gate: bfloat16 [2048, 1024], P('dp'), may hold values from -0.125 to 0.125
- w_up: bfloat16 [2048, 1024], P('dp'), may hold values from -0.125 to 0.125
- w_down: bfloat16 [2048, 1024], P('dp'), may hold values from -0.1875 to 0.1875
Outputs:
- mixed: bfloat16 [73728, 2048], P('dp')
- token_grad: bfloat16 [73728, 2048], P('dp')
- grad_gate: float32 [2048, 1024], P('dp')
- grad_up: float32 [2048, 1024], P('dp')
- grad_down: float32 [2048, 1024], P('dp')
Inputs may be any that keep to these rules, and one draw needn't show every extreme that they name: row_count sums to 192 * the number of devices; rows beyond a device's count are not part of its micro-batch.
All inputs are finite; a program needn't handle non-finite values.
Results may differ from a plain program's by a relative error of at most 0.0057.
Values may be sent and summed in bfloat16 or wider, within the bound.
A program may use at most 192 MiB of HBM per device.

v0:
```python
import jax
import jax.numpy as jnp
from jax import lax
from jax.sharding import PartitionSpec as P


def contract_rows(left_part, right_part):
    return lax.dot_general(
        left_part, right_part, (((0,), (0,)), ((), ())), preferred_element_type=jnp.float32
    )


def contract_cols(left_part, right_part):
    return lax.dot_general(
        left_part, right_part, (((1,), (1,)), ((), ())), preferred_element_type=jnp.float32
    )


def expert_rows(rows_in, row_gain, cot_rows, gate_full, up_full, down_full):
    gain_col = row_gain.astype(jnp.float32)[:, None]
    gate_pre = jnp.dot(rows_in, gate_full, preferred_element_type=jnp.float32)
    up_pre = jnp.dot(rows_in, up_full, preferred_element_type=jnp.float32)
    sigma_gate = jax.nn.sigmoid(gate_pre)
    silu_gate = gate_pre * sigma_gate
    hidden = (silu_gate * up_pre).astype(jnp.bfloat16)
    projected = contract_cols(hidden, down_full)
    mixed = (gain_col * projected).astype(jnp.bfloat16)
    out_grad = (gain_col * cot_rows.astype(jnp.float32)).astype(jnp.bfloat16)
    act_grad = jnp.dot(out_grad, down_full, preferred_element_type=jnp.float32)
    gate_grad = (act_grad * up_pre * sigma_gate * (1.0 + gate_pre * (1.0 - sigma_gate))).astype(
        jnp.bfloat16
    )
    up_grad = (act_grad * silu_gate).astype(jnp.bfloat16)
    token_grad = (contract_cols(gate_grad, gate_full) + contract_cols(up_grad, up_full)).astype(
        jnp.bfloat16
    )
    return (mixed, token_grad, gate_grad, up_grad, out_grad, hidden)


def body(tokens, route_gate, cotangent, row_count, w_gate, w_up, w_down):
    row_slots = tokens.shape[0]
    gate_full, up_full, down_full = (
        lax.all_gather(w_gate, "dp", axis=0, tiled=True),
        lax.all_gather(w_up, "dp", axis=0, tiled=True),
        lax.all_gather(w_down, "dp", axis=0, tiled=True),
    )
    live_row = jnp.arange(row_slots, dtype=jnp.int32) < row_count[0]
    row_gain = jnp.where(live_row, route_gate, jnp.zeros_like(route_gate))
    mixed, token_grad, gate_grad, up_grad, out_grad, hidden = expert_rows(
        tokens, row_gain, cotangent, gate_full, up_full, down_full
    )
    grad_terms = lax.psum_scatter(
        jnp.concatenate(
            [
                contract_rows(tokens, gate_grad),
                contract_rows(tokens, up_grad),
                contract_rows(out_grad, hidden),
            ],
            axis=1,
        ),
        "dp",
        scatter_dimension=0,
        tiled=True,
    )
    hidden_width = w_gate.shape[1]
    return (
        mixed,
        token_grad,
        grad_terms[:, :hidden_width],
        grad_terms[:, hidden_width : 2 * hidden_width],
        grad_terms[:, 2 * hidden_width :],
    )


def solution(mesh):
    placed = (
        P("dp", None),
        P("dp"),
        P("dp", None),
        P("dp"),
        P("dp", None),
        P("dp", None),
        P("dp", None),
    )
    return jax.shard_map(
        body,
        mesh=mesh,
        in_specs=placed,
        out_specs=(P("dp", None), P("dp", None), P("dp", None), P("dp", None), P("dp", None)),
        check_vma=False,
    )
```

profile of v0, /device:TPU:0, one launch (start us, length us, event | category | flops | bytes accessed | tf_op | source)
XLA Modules:
  0.0 522.1 jit_solution(13897330379130603873)
XLA Ops:
  7.2 0.0 copy-start
  7.2 0.0 all-gather.6.cloned.1.call-start
  7.2 0.7 all-gather.6.cloned.1.call-update
  7.9 0.0 all-gather.4.cloned.1.call-start
  8.0 0.7 all-gather.4.cloned.1.call-update
  8.7 0.0 all-gather.8.cloned.1.call-start
  8.7 0.7 all-gather.8.cloned.1.call-update
  9.4 0.0 reduce-scatter.4.cloned.1.call-start
  10.1 0.7 fusion.4
  10.8 69.8 %all-gather.6.cloned.1.call-done = bf16[2048,1024]{1,0:T(8,128)(2,1)} async-done(((bf16[16,1024]{1,0:T(8,128)(2,1)}), bf16[2048,1024]{1,0:T(8,128)(2,1)}) %all-gather.6.cloned.1.call-update) | async-done | bytes 4194320 | tf_op jit(solution)/shard_map/all_gather | solution.py:44
  80.6 0.0 copy-done
  80.6 6.2 %fusion.7 = f32[576,1024]{1,0:T(8,128)} fusion(bf16[576,2048]{1,0:T(8,128)(2,1)S(1)} %copy-done, bf16[2048,1024]{1,0:T(8,128)(2,1)} %all-gather.6.cloned.1.call-done), kind=kOutput, calls=%fused_computation.18 | convolution fusion | flops 2415919104 | bytes 8912896 | tf_op jit(solution)/shard_map/dot_general | solution.py:22
  86.8 61.4 %all-gather.4.cloned.1.call-done = bf16[2048,1024]{1,0:T(8,128)(2,1)} async-done(((bf16[16,1024]{1,0:T(8,128)(2,1)}), bf16[2048,1024]{1,0:T(8,128)(2,1)}) %all-gather.4.cloned.1.call-update) | async-done | bytes 4194320 | tf_op jit(solution)/shard_map/all_gather | solution.py:43
  148.1 6.2 %fusion.6 = f32[576,1024]{1,0:T(8,128)} fusion(bf16[576,2048]{1,0:T(8,128)(2,1)S(1)} %copy-done, bf16[2048,1024]{1,0:T(8,128)(2,1)} %all-gather.4.cloned.1.call-done), kind=kOutput, calls=%fused_computation.17 | convolution fusion | flops 2415919104 | bytes 8912896 | tf_op jit(solution)/shard_map/dot_general | solution.py:21
  154.3 61.4 %all-gather.8.cloned.1.call-done = bf16[2048,1024]{1,0:T(8,128)(2,1)} async-done(((bf16[16,1024]{1,0:T(8,128)(2,1)}), bf16[2048,1024]{1,0:T(8,128)(2,1)}) %all-gather.8.cloned.1.call-update) | async-done | bytes 4194320 | tf_op jit(solution)/shard_map/all_gather | solution.py:45
  215.7 7.7 %multiply_convert_fusion.2 = (bf16[576,1024]{1,0:T(8,128)(2,1)S(1)}, bf16[576,1024]{1,0:T(8,128)(2,1)S(1)}, bf16[576,1024]{1,0:T(8,128)(2,1)S(1)}) fusion(f32[576,1024]{1,0:T(8,128)} %fusion.6, f32[576,1024]{1,0:T(8,128)} %fusion.7, bf16[2048,1024]{1,0:T(8,128)(2,1)} %all-gather.8.cloned.1.call-done, bf16[576,2048]{1,0:T(8,128)(2,1)} %param.9, ...), kind=kOutput, calls=%fused_computation.6 | convolution fusion | flops 2428305408 | bytes 14813440 | tf_op jit(solution)/shard_map/dot_general | solution.py:29
  223.4 0.0 copy-start.5
  223.4 0.0 copy-start.7
  223.5 3.5 convolution_bitcast_fusion
  226.9 0.0 copy-done.5
  226.9 0.0 copy-done.7
  227.0 0.0 copy-start.4
  227.0 3.7 convolution_bitcast_fusion.1
  230.6 0.0 copy-done.4
  230.7 3.6 fusion.1
  234.2 10.6 %pad_maximum_fusion = f32[2048,3072]{0,1:T(8,128)} fusion(f32[2048,1024]{0,1:T(8,128)S(1)} %fusion.1, f32[2048,1024]{0,1:T(8,128)S(1)} %convolution_bitcast_fusion, f32[2048,1024]{0,1:T(8,128)S(1)} %convolution_bitcast_fusion.1), kind=kLoop, calls=%fused_computation | loop fusion | flops 12582912 | bytes 50331648 | tf_op jit(solution)/shard_map/concatenate | solution.py:53
  244.8 24.7 %copy.18 = f32[2048,3072]{1,0:T(8,128)} copy(f32[2048,3072]{0,1:T(8,128)} %pad_maximum_fusion) | data formatting | bytes 50331648
  269.6 0.0 copy-start.8
  269.6 0.0 reduce-scatter.4.cloned.1.call-update
  269.6 1.2 copy-done.8
  270.8 0.0 copy-start.3
  270.8 4.6 fusion.8
  275.4 0.0 copy-done.3
  275.5 0.0 copy-start.2
  275.5 0.0 copy-start.6
  275.5 3.9 multiply_convert_fusion.1
  279.4 0.0 copy-done.2
  279.4 0.0 copy-done.6
  279.4 0.0 copy-start.1
  279.4 3.9 add_convert_fusion
  283.3 230.6 %reduce-scatter.4.cloned.1.call-done = f32[16,3072]{1,0:T(8,128)} async-done(((f32[2048,3072]{1,0:T(8,128)}), f32[16,3072]{1,0:T(8,128)}) %reduce-scatter.4.cloned.1.call-update) | async-done | bytes 196624
  513.9 1.6 fusion.5
  515.5 0.0 copy-done.1
Async XLA Ops:
  7.2 73.4 %copy-start = (bf16[576,2048]{1,0:T(8,128)(2,1)S(1)}, bf16[576,2048]{1,0:T(8,128)(2,1)}, u32[]{:S(2)}) copy-start(bf16[576,2048]{1,0:T(8,128)(2,1)} %param.7) | copy-start | bytes 7077892
  7.2 73.4 %all-gather.6.cloned.1.call-start = ((), (), s32[]{:S(2)}) async-start(), calls=%async_computation.2 | async-start | bytes 4227072 | tf_op jit(solution)/shard_map/all_gather | solution.py:44
  7.9 140.2 %all-gather.4.cloned.1.call-start = ((), (), s32[]{:S(2)}) async-start(), calls=%async_computation.1 | async-start | bytes 4227072 | tf_op jit(solution)/shard_map/all_gather | solution.py:43
  8.7 207.0 %all-gather.8.cloned.1.call-start = ((), (), s32[]{:S(2)}) async-start(), calls=%async_computation.3 | async-start | bytes 4227072 | tf_op jit(solution)/shard_map/all_gather | solution.py:45
  9.4 504.5 %reduce-scatter.4.cloned.1.call-start = ((), (), s32[]{:S(2)}) async-start(), calls=%async_computation.4 | async-start | bytes 25362432
  223.4 3.5 copy-start.5
  223.4 3.5 copy-start.7
  227.0 3.7 copy-start.4
  269.6 1.3 copy-start.8
  270.8 4.6 copy-start.3
  275.5 3.9 copy-start.2
  275.5 3.9 copy-start.6
  279.4 236.1 %copy-start.1 = (bf16[576,2048]{1,0:T(8,128)(2,1)S(1)}, bf16[576,2048]{1,0:T(8,128)(2,1)}, u32[]{:S(2)}) copy-start(bf16[576,2048]{1,0:T(8,128)(2,1)} %param.7) | copy-start | bytes 7077892
Sparse Core Ops, SparseCore 0:
  11.2 69.3 all-gather.5
  83.7 64.3 all-gather.3
  151.3 64.3 all-gather.7
  269.7 244.1 reduce-scatter.3
where the time goes:
time: 523 us; the launch traced here: 522 us
  waiting for transfers between devices  425 us (81%)
  matrix products  43.3 us (8%)
  local copies, waits for them, and re-layouts  27.6 us (5%)
  between operations  14.5 us (3%)
  other arithmetic  11.3 us (2%)
    unnamed x5, waiting for transfers between devices  233 us
    all_gather x1, waiting for transfers between devices, body(): lax.all_gather(w_up, 'dp', axis=0, tiled=True)  69.8 us
    all_gather x1, waiting for transfers between devices, body(): lax.all_gather(w_down, 'dp', axis=0, tiled=True)  61.4 us
    all_gather x1, waiting for transfers between devices, body(): lax.all_gather(w_gate, 'dp', axis=0, tiled=True)  61.4 us
    unnamed x19, local copies, waits for them, and re-layouts  26 us
    dot_general x3, matrix products, contract_cols(): lax.dot_general(left_part, right_part, (((1,), (1,)), ((), ())), preferre...  12.4 us
    dot_general x3, matrix products, contract_rows(): lax.dot_general(left_part, right_part, (((0,), (0,)), ((), ())), preferre...  10.7 us
    concatenate x1, other arithmetic, body(): jnp.concatenate([contract_rows(tokens, gate_grad), contract_rows(tokens,...  10.6 us
  transfers between devices with their start and end apart: 4, of which 4 were waited for; matrix products, arithmetic and copies ran while one was open for 5% of the time, Pallas kernels for 0%

commit v1 on v0

v1 whole, which is shorter than its diff:
```python
import functools

import jax
import jax.numpy as jnp
from jax import lax
from jax.experimental import pallas as pl
from jax.experimental.pallas import tpu as pltpu
from jax.sharding import PartitionSpec as P

bf16 = jnp.bfloat16
f32 = jnp.float32
H = 2
NT = (((1,), (1,)), ((), ()))
ORDER = ((32, 4, 1), (1, 32, 4), (4, 1, 32))


def place(p, d):
    y, x, z, core = d // 32, d // 8 % 4, d // 2 % 4, d % 2
    k = y * ORDER[p][0] + x * ORDER[p][1] + z * ORDER[p][2]
    return 16 * (k // 32 * 32 + core * 16 + k % 32)


def stride(p):
    return 32 - 33 * p + 9 * p * p


def al(v, n=16):
    return pl.multiple_of(v, n)


def kernel(
    tok_in, cot_in, gain_in, wg_in, wu_in, wd_in,
    mixed, tgrad, out_g, out_u, out_d,
    tok, og, gain, wt, lt, acc, gr, part, sd, rd, cr, br, ar,
    loc, ss, ra, rb, rc, rf, rdg, dS, dR, cS, cR, bS, bR, aS, aR,
):
    F = wt.shape[2]
    me = lax.axis_index("dp")
    core = me % 2
    sib = me + 1 - 2 * core

    def coord(p):
        return me // stride(p) % 4

    def dev(p, r):
        s = stride(p)
        k = me // s % 4
        return me + ((k + r) % 4 - k) * s

    def ax(p):
        return p, (p + 1) % 3, (p + 2) % 3

    def rcopy(src, dst, ssem, rsem, to):
        c = pltpu.make_async_remote_copy(
            src_ref=src, dst_ref=dst, send_sem=ssem, recv_sem=rsem,
            device_id=(to,), device_id_type=pl.DeviceIdType.MESH)
        c.start()

    def got(ref, sem):
        pltpu.make_async_copy(ref, ref, sem).wait()

    def each(fn):
        def step(p, _):
            fn(p)
            return 0
        lax.fori_loop(0, 3, step, 0)

    own = [me // 32 * wy + me // 8 % 4 * wx + me // 2 % 4 * wz for wy, wx, wz in ORDER]
    own = [al(16 * (k // 32 * 32 + core * 16 + k % 32)) for k in own]
    cps = []
    for h in range(H):
        for p, w in enumerate((wg_in, wu_in, wd_in)):
            cps.append(pltpu.make_async_copy(
                w.at[:, pl.ds(h * F, F)], wt.at[h * 3 + p, pl.ds(own[p], 16)], loc.at[h * 3 + p]))
    big = [pltpu.make_async_copy(tok_in, tok, loc.at[6]),
           pltpu.make_async_copy(cot_in, og, loc.at[7]),
           pltpu.make_async_copy(gain_in, gain, loc.at[8])]
    for c in cps + big:
        c.start()

    bar = pltpu.get_barrier_semaphore()
    for p in range(3):
        for r in (1, 2, 3):
            pl.semaphore_signal(bar, inc=1, device_id=(dev(p, r),), device_id_type=pl.DeviceIdType.MESH)
    pl.semaphore_signal(bar, inc=1, device_id=(sib,), device_id_type=pl.DeviceIdType.MESH)
    pl.semaphore_wait(bar, 10)
    for c in cps:
        c.wait()

    def base(p):
        sl, mi, fa = ax(p)
        return coord(sl), coord(mi), coord(fa)

    def ag_a(h):
        def fn(p):
            kc, kb, ka = base(p)
            hp = h * 3 + p
            blk = wt.at[hp, pl.ds(al(kc * 512 + core * 256 + kb * 64 + ka * 16), 16)]
            for r in (1, 2, 3):
                rcopy(blk, blk, ss.at[hp], ra.at[hp], dev(ax(p)[2], r))
        each(fn)

    def line(p, hp, kb):
        return wt.at[hp, pl.ds(al(coord(p) * 512 + core * 256 + kb * 64, 64), 64)]

    def send_line(p, hp, kb):
        ref = line(p, hp, kb)
        half = kb // 2
        rcopy(ref, ref, ss.at[hp], rc.at[hp * 4 + half], dev(p, 1))
        rcopy(ref, ref, ss.at[hp], rc.at[hp * 4 + 2 + half], dev(p, 3))

    def ag_b(h):
        def fn(p):
            hp = h * 3 + p
            kb = coord(ax(p)[1])
            got(wt.at[hp, pl.ds(0, 48)], ra.at[hp])
            ref = line(p, hp, kb)
            for r in (1, 2, 3):
                rcopy(ref, ref, ss.at[hp], rb.at[hp], dev(ax(p)[1], r))
            send_line(p, hp, kb)
        each(fn)

    def plane(hp, kc):
        return wt.at[hp, pl.ds(al(kc * 512 + core * 256, 256), 256)]

    def to_sib(p, hp, r):
        ref = plane(hp, (coord(p) + r) % 4)
        rcopy(ref, ref, ss.at[hp], rdg.at[hp * 4 + r], sib)

    def ag_c(h):
        def fn(p):
            hp = h * 3 + p
            kb = coord(ax(p)[1])
            got(wt.at[hp, pl.ds(0, 192)], rb.at[hp])
            for j in (1, 2, 3):
                send_line(p, hp, (kb + j) % 4)
            to_sib(p, hp, 0)
        each(fn)

    def ag_f(h):
        def fn(p):
            hp = h * 3 + p
            low = wt.at[hp, pl.ds(0, 128)]
            got(low, rc.at[hp * 4])
            src = wt.at[hp, pl.ds(al((coord(p) + 3) % 4 * 512 + core * 256, 256), 128)]
            rcopy(src, src, ss.at[hp], rf.at[hp * 2], dev(p, 1))
            got(low, rc.at[hp * 4 + 3])
            src = wt.at[hp, pl.ds(al((coord(p) + 1) % 4 * 512 + core * 256 + 128, 128), 128)]
            rcopy(src, src, ss.at[hp], rf.at[hp * 2 + 1], dev(p, 3))
            got(low, rc.at[hp * 4 + 1])
            to_sib(p, hp, 3)
            got(low, rc.at[hp * 4 + 2])
            to_sib(p, hp, 1)
        each(fn)

    def ag_g(h):
        def fn(p):
            hp = h * 3 + p
            got(wt.at[hp, pl.ds(0, 128)], rf.at[hp * 2])
            got(wt.at[hp, pl.ds(0, 128)], rf.at[hp * 2 + 1])
            to_sib(p, hp, 2)
        each(fn)

    def ag_wait(h, p):
        hp = h * 3 + p
        for r in range(4):
            got(plane(hp, r), rdg.at[hp * 4 + r])

    eye = (lax.broadcasted_iota(jnp.int32, (256, 256), 0)
           == lax.broadcasted_iota(jnp.int32, (256, 256), 1)).astype(f32).astype(bf16)

    def turn(src, ps):
        def step(t, _):
            cols = pl.ds(al(t * 256, 256), 256)
            v = lax.dot_general(eye, src[:, cols], NT, preferred_element_type=f32).astype(bf16)
            for p in ps:
                for j in range(16):
                    y, x, z, c = t // 2, t % 2 * 2 + j // 8, j // 2 % 4, j % 2
                    wy, wx, wz = ORDER[p]
                    k = y * wy + x * wx + z * wz
                    row = 16 * (k // 32 * 32 + c * 16 + k % 32)
                    lt[p, pl.ds(al(row), 16), :] = v[j * 16:(j + 1) * 16]
            return 0
        lax.fori_loop(0, 8, step, 0)

    def scale():
        def step(i, _):
            s = pl.ds(al(i * 32, 32), 32)
            g = gain[s, 0:1]
            og[s, :] = (g * og[s, :].astype(f32)).astype(bf16)
            return 0
        lax.fori_loop(0, 18, step, 0)

    def nn(h, p):
        w = jnp.concatenate([wt[h * 3 + p, pl.ds(place(p, d), 16), :] for d in range(128)], axis=0)
        lhs = og if p == 2 else tok
        acc[p] = jnp.dot(lhs[...], w, preferred_element_type=f32)

    def act(h):
        def step(i, _):
            s = pl.ds(al(i * 64, 64), 64)
            g, u, a = acc[0, s, :], acc[1, s, :], acc[2, s, :]
            sg = jax.nn.sigmoid(g)
            si = g * sg
            gr[h * 3 + 2, s, :] = (si * u).astype(bf16)
            gr[h * 3, s, :] = (a * u * sg * (1.0 + g * (1.0 - sg))).astype(bf16)
            gr[h * 3 + 1, s, :] = (a * si).astype(bf16)
            return 0
        lax.fori_loop(0, 9, step, 0)

    def rs_dot(h, r):
        def fn(q):
            hq = h * 3 + q
            row = (coord(q) + r) % 4 * 512
            mine = lt[q, pl.ds(al(row + core * 256, 256), 256), :]
            theirs = lt[q, pl.ds(al(row + 256 - core * 256, 256), 256), :]
            v = jnp.dot(jnp.concatenate([theirs, mine], axis=0), gr[hq], preferred_element_type=f32)
            sd[q * 4 + r] = v[0:256].astype(bf16)
            rcopy(sd.at[q * 4 + r], rd.at[hq * 4 + r], dS.at[hq * 4 + r], dR.at[hq * 4 + r], sib)
            part[q * 4 + r] = v[256:512]
        each(fn)

    def sd_done(h):
        def fn(q):
            for r in range(4):
                got(sd.at[q * 4 + r], dS.at[(h * 3 + q) * 4 + r])
        each(fn)

    def rs_far(h):
        def fn(q):
            hq = h * 3 + q
            far = rd.at[hq * 4 + 2]
            got(far, dR.at[hq * 4 + 2])
            far[...] = (part[q * 4 + 2] + far[...].astype(f32)).astype(bf16)
            lo, hi = pl.ds(0, 128), pl.ds(128, 128)
            rcopy(far.at[lo], cr.at[hq * 3, lo], cS.at[hq * 4], cR.at[hq * 4], dev(q, 1))
            rcopy(far.at[hi], cr.at[hq * 3, hi], cS.at[hq * 4 + 1], cR.at[hq * 4 + 1], dev(q, 3))
        each(fn)

    def rs_near(h, r):
        i, thru, rest = (0, pl.ds(0, 128), pl.ds(128, 128)) if r == 1 else (1, pl.ds(128, 128), pl.ds(0, 128))

        def fn(q):
            hq = h * 3 + q
            near = rd.at[hq * 4 + r]
            got(near, dR.at[hq * 4 + r])
            near[rest, :] = (part[q * 4 + r, rest, :] + near[rest, :].astype(f32)).astype(bf16)
            got(cr.at[hq * 3, thru], cR.at[hq * 4 + i])
            near[thru, :] = (part[q * 4 + r, thru, :] + near[thru, :].astype(f32)
                             + cr[hq * 3, thru, :].astype(f32)).astype(bf16)
            rcopy(near, cr.at[hq * 3 + 1 + i], cS.at[hq * 4 + 2 + i], cR.at[hq * 4 + 2 + i], dev(q, r))
        each(fn)

    def rs_b(h):
        def fn(q):
            hq = h * 3 + q
            mid = rd.at[hq * 4]
            got(mid, dR.at[hq * 4])
            got(cr.at[hq * 3 + 1], cR.at[hq * 4 + 2])
            got(cr.at[hq * 3 + 2], cR.at[hq * 4 + 3])
            v = (part[q * 4] + mid[...].astype(f32)
                 + cr[hq * 3 + 1].astype(f32) + cr[hq * 3 + 2].astype(f32))
            part[q * 4] = v
            mid[...] = v.astype(bf16)
            b = ax(q)[1]
            kb = coord(b)
            for r in (1, 2, 3):
                rcopy(mid.at[pl.ds(al((kb + r) % 4 * 64, 64), 64)], br.at[hq, pl.ds((r - 1) * 64, 64)],
                      bS.at[hq], bR.at[hq], dev(b, r))
        each(fn)

    def rs_a(h):
        def fn(q):
            hq = h * 3 + q
            _, b, a = ax(q)
            row = al(coord(b) * 64, 64)
            mine = pl.ds(row, 64)
            got(br.at[hq], bR.at[hq])
            v = part[q * 4, mine, :]
            for r in range(3):
                v = v + br[hq, pl.ds(r * 64, 64), :].astype(f32)
            part[q * 4, mine, :] = v
            rd[hq * 4, mine, :] = v.astype(bf16)
            for r in (1, 2, 3):
                rcopy(rd.at[hq * 4, pl.ds(al(row + (coord(a) + r) % 4 * 16), 16)], ar.at[hq, pl.ds((r - 1) * 16, 16)],
                      aS.at[hq], aR.at[hq], dev(a, r))
        each(fn)

    def rs_end(h):
        for q, out in enumerate((out_g, out_u, out_d)):
            hq = h * 3 + q
            _, b, a = ax(q)
            got(ar.at[hq], aR.at[hq])
            v = part[q * 4, pl.ds(al(coord(b) * 64 + coord(a) * 16), 16), :]
            for r in range(3):
                v = v + ar[hq, pl.ds(r * 16, 16), :].astype(f32)
            out[:, h * F:(h + 1) * F] = v

    def rows_out(t0, t1):
        def step(t, _):
            def nat(hp, p):
                wy, wx, wz = ORDER[p]
                ps = []
                for j in range(32):
                    x, z, c = j // 8, j // 2 % 4, j % 2
                    k = t * wy + x * wx + z * wz
                    ps.append(wt[hp, pl.ds(al(16 * (k // 32 * 32 + c * 16 + k % 32)), 16), :])
                return jnp.concatenate(ps, axis=0)
            cols = pl.ds(al(t * 512, 512), 512)
            m = g = None
            for h in range(H):
                d = lax.dot_general(gr[h * 3 + 2], nat(h * 3 + 2, 2), NT, preferred_element_type=f32)
                m = d if m is None else m + d
            mixed[:, cols] = (gain[:, 0:1] * m).astype(bf16)
            for h in range(H):
                for p in (0, 1):
                    d = lax.dot_general(gr[h * 3 + p], nat(h * 3 + p, p), NT, preferred_element_type=f32)
                    g = d if g is None else g + d
            tgrad[:, cols] = g.astype(bf16)
            return 0
        lax.fori_loop(t0, t1, step, 0)

    ag_a(0)
    ag_a(1)
    big[0].wait()
    ag_b(0)
    turn(tok, (0, 1))
    ag_c(0)
    ag_b(1)
    big[1].wait()
    big[2].wait()
    scale()
    turn(og, (2,))
    ag_c(1)
    ag_f(0)
    ag_g(0)
    for p in range(3):
        ag_wait(0, p)
        nn(0, p)
        if p == 1:
            ag_f(1)
    act(0)
    rs_dot(0, 2)
    ag_g(1)
    rs_far(0)
    rs_dot(0, 1)
    rs_dot(0, 3)
    rs_near(0, 1)
    rs_near(0, 3)
    rs_dot(0, 0)
    for p in range(3):
        ag_wait(1, p)
        nn(1, p)
    act(1)
    sd_done(0)
    rs_dot(1, 2)
    rs_b(0)
    rs_far(1)
    rs_dot(1, 1)
    rs_dot(1, 3)
    rs_a(0)
    rs_near(1, 1)
    rs_near(1, 3)
    rs_end(0)
    rs_dot(1, 0)
    rows_out(0, 2)
    rs_b(1)
    rows_out(2, 3)
    rs_a(1)
    rows_out(3, 4)
    rs_end(1)

    sd_done(1)
    for hp in range(3 * H):
        got(wt.at[hp, pl.ds(0, 2032)], ss.at[hp])
        got(rd.at[hp, pl.ds(0, 128)], cS.at[hp * 4])
        got(rd.at[hp, pl.ds(0, 128)], cS.at[hp * 4 + 1])
        got(rd.at[hp], cS.at[hp * 4 + 2])
        got(rd.at[hp], cS.at[hp * 4 + 3])
        got(br.at[hp], bS.at[hp])
        got(ar.at[hp], aS.at[hp])


def body(tokens, route_gate, cotangent, row_count, w_gate, w_up, w_down):
    rows, width = tokens.shape
    ff = w_gate.shape[1]
    F = ff // H
    live = jnp.arange(rows, dtype=jnp.int32) < row_count[0]
    gain = jnp.where(live, route_gate, jnp.zeros_like(route_gate)).astype(f32)
    gain = jnp.broadcast_to(gain[:, None], (rows, 128))
    anyspace = pl.BlockSpec(memory_space=pl.ANY)
    vmem = pl.BlockSpec(memory_space=pltpu.VMEM)
    dma = pltpu.SemaphoreType.DMA
    n = 3 * H
    return pl.pallas_call(
        kernel,
        out_shape=(
            jax.ShapeDtypeStruct((rows, width), bf16),
            jax.ShapeDtypeStruct((rows, width), bf16),
            jax.ShapeDtypeStruct((16, ff), f32),
            jax.ShapeDtypeStruct((16, ff), f32),
            jax.ShapeDtypeStruct((16, ff), f32),
        ),
        in_specs=[anyspace] * 6,
        out_specs=[vmem] * 5,
        scratch_shapes=[
            pltpu.VMEM((rows, width), bf16),
            pltpu.VMEM((rows, width), bf16),
            pltpu.VMEM((rows, 128), f32),
            pltpu.VMEM((n, width, F), bf16),
            pltpu.VMEM((3, width, rows), bf16),
            pltpu.VMEM((3, rows, F), f32),
            pltpu.VMEM((n, rows, F), bf16),
            pltpu.VMEM((12, 256, F), f32),
            pltpu.VMEM((12, 256, F), bf16),
            pltpu.VMEM((n * 4, 256, F), bf16),
            pltpu.VMEM((n * 3, 256, F), bf16),
            pltpu.VMEM((n, 192, F), bf16),
            pltpu.VMEM((n, 48, F), bf16),
            dma((9,)), dma((n,)), dma((n,)), dma((n,)), dma((n * 4,)), dma((n * 2,)), dma((n * 4,)),
            dma((n * 4,)), dma((n * 4,)), dma((n * 4,)), dma((n * 4,)),
            dma((n,)), dma((n,)), dma((n,)), dma((n,)),
        ],
        compiler_params=pltpu.CompilerParams(
            collective_id=0, has_side_effects=True, vmem_limit_bytes=64 * 1024 * 1024 - 65536),
        cost_estimate=pl.CostEstimate(
            flops=18 * rows * width * ff, bytes_accessed=8 * rows * width, transcendentals=rows * ff),
    )(tokens, cotangent, gain, w_gate, w_up, w_down)


def solution(mesh):
    row, vec = P("dp", None), P("dp")
    return jax.shard_map(
        body,
        mesh=mesh,
        in_specs=(row, vec, row, vec, row, row, row),
        out_specs=(row,) * 5,
        check_vma=False,
    )
```

time: 523 us -> 95 us (0.18)
  waiting for transfers between devices: 425 us -> 0 us
  Pallas kernels: 0 us -> 85.2 us
  matrix products: 43.3 us -> 0 us
  local copies, waits for them, and re-layouts: 27.6 us -> 7.68 us
  between operations: 14.5 us -> 1.3 us
  other arithmetic: 11.3 us -> 0.69 us
    unnamed x5 -> x0, waiting for transfers between devices: 233 us -> none
    all_gather x3 -> x0, waiting for transfers between devices: 193 us -> none  [the longest x1 69.8 us: body(): lax.all_gather(w_up, 'dp', axis=0, tiled=True)]
    pallas_call x0 -> x1, Pallas kernels: none -> 85.2 us  [body(): pl.pallas_call(kernel, out_shape=(jax.ShapeDtypeStruct((rows, width), bf1...]
    dot_general x9 -> x0, matrix products: 43.3 us -> none  [the longest x3 12.4 us: contract_cols(): lax.dot_general(left_part, right_part, (((1,), (1,)), ((), ())), preferre...]
    unnamed x19 -> x13, local copies, waits for them, and re-layouts: 26 us -> 6.82 us
    concatenate x1 -> x0, other arithmetic: 10.6 us -> none  [body(): jnp.concatenate([contract_rows(tokens, gate_grad), contract_rows(tokens,...]
  transfers between devices with their start and end apart: 4 -> 0, of which waited for: 4 -> 0; matrix products, arithmetic and copies ran while one was open for 5% -> 0% of each run, Pallas kernels for 0% -> 0%
where the time goes in v1:
time: 95 us; the launch traced here: 94.9 us
  Pallas kernels  85.2 us (90%)
  local copies, waits for them, and re-layouts  7.68 us (8%)
  between operations  1.3 us (1%)
    pallas_call x1, Pallas kernels, body(): pl.pallas_call(kernel, out_shape=(jax.ShapeDtypeStruct((rows, width), bf1...  85.2 us
    unnamed x13, local copies, waits for them, and re-layouts  6.82 us

profile of v1, /device:TPU:0, one launch (start us, length us, event | category | flops | bytes accessed | tf_op | source)
XLA Modules:
  0.0 94.9 jit_solution(5155161613443025611)
XLA Ops:
  1.3 0.7 fusion.1
  2.0 0.9 broadcast_in_dim.10.gain_in
  2.8 85.2 %shard_map.110 = (bf16[576,2048]{1,0:T(8,128)(2,1)}, bf16[576,2048]{1,0:T(8,128)(2,1)}, f32[16,1024]{1,0:T(8,128)}, f32[16,1024]{1,0:T(8,128)}, f32[16,1024]{1,0:T(8,128)}) custom-call(bf16[576,2048]{1,0:T(8,128)(2,1)} %tok_in.1, bf16[576,2048]{1,0:T(8,128)(2,1)} %cot_in.1, f32[576,128]{1,0:T(8,128)} %broadcast_in_dim.10.gain_in, bf16[16,1024]{1,0:T(8,128)(2,1)} %wg_in.1, ...), custom_call_target="tpu_custom_call" | custom-call | flops 21743271936 | bytes 9437184 | tf_op jit(solution)/shard_map/pallas_call | solution.py:395
  88.0 0.0 copy-start
  88.0 3.5 %copy.18 = bf16[576,2048]{1,0:T(8,128)(2,1)} copy(bf16[576,2048]{1,0:T(8,128)(2,1)} %get-tuple-element.10) | data formatting | bytes 4718592
  91.6 0.0 copy-done
  91.6 0.0 copy-start.3
  91.6 0.0 copy-start.2
  91.6 0.0 copy-start.1
  91.6 1.4 %copy.19 = bf16[576,2048]{1,0:T(8,128)(2,1)} copy(bf16[576,2048]{1,0:T(8,128)(2,1)S(1)} %copy-done) | data formatting | bytes 4718592
  93.0 0.0 copy-done.3
  93.0 0.6 copy.20
  93.6 0.0 copy-done.2
  93.6 0.6 copy.21
  94.2 0.0 copy-done.1
  94.2 0.6 copy.22
Async XLA Ops:
  88.0 3.5 %copy-start = (bf16[576,2048]{1,0:T(8,128)(2,1)S(1)}, bf16[576,2048]{1,0:T(8,128)(2,1)}, u32[]{:S(2)}) copy-start(bf16[576,2048]{1,0:T(8,128)(2,1)} %get-tuple-element.11) | copy-start | bytes 7077892
  91.6 1.4 %copy-start.3 = (f32[16,1024]{1,0:T(8,128)S(1)}, f32[16,1024]{1,0:T(8,128)}, u32[]{:S(2)}) copy-start(f32[16,1024]{1,0:T(8,128)} %get-tuple-element.12) | copy-start | bytes 196612
  91.6 2.1 %copy-start.2 = (f32[16,1024]{1,0:T(8,128)S(1)}, f32[16,1024]{1,0:T(8,128)}, u32[]{:S(2)}) copy-start(f32[16,1024]{1,0:T(8,128)} %get-tuple-element.13) | copy-start | bytes 196612
  91.6 2.7 %copy-start.1 = (f32[16,1024]{1,0:T(8,128)S(1)}, f32[16,1024]{1,0:T(8,128)}, u32[]{:S(2)}) copy-start(f32[16,1024]{1,0:T(8,128)} %get-tuple-element.14) | copy-start | bytes 196612

commit v2 on v1

v2 whole, which is shorter than its diff:
```python
import functools

import jax
import jax.numpy as jnp
from jax import lax
from jax.experimental import pallas as pl
from jax.experimental.pallas import tpu as pltpu
from jax.sharding import PartitionSpec as P

bf16 = jnp.bfloat16
f32 = jnp.float32
H = 4
NT = (((1,), (1,)), ((), ()))
ORDER = ((32, 4, 1), (1, 32, 4), (4, 1, 32))


def place(p, d):
    y, x, z, core = d // 32, d // 8 % 4, d // 2 % 4, d % 2
    k = y * ORDER[p][0] + x * ORDER[p][1] + z * ORDER[p][2]
    return 16 * (k // 32 * 32 + core * 16 + k % 32)


def al(v, n=16):
    return pl.multiple_of(v, n)


def kernel(
    tok_in, cot_in, gate_in, count, wg_in, wu_in, wd_in,
    mixed, tgrad, out_g, out_u, out_d,
    tok, og, gain, wt, lt, acc, gr, part, sd, rd, cr, br, ar,
    loc, ss, ra, rb, rc, rf, rdg, dS, dR, cS, cR, bS, bR, aS, aR,
):
    F = wt.shape[2]
    me = lax.axis_index("dp")
    core = me % 2
    sib = me + 1 - 2 * core

    pos = (me // 32, me // 8 % 4, me // 2 % 4)
    peer = [[me + ((pos[p] + r) % 4 - pos[p]) * st for r in range(4)] for p, st in enumerate((32, 8, 2))]

    def coord(p):
        return pos[p]

    def dev(p, r):
        return peer[p][r]

    def ax(p):
        return p, (p + 1) % 3, (p + 2) % 3

    def rcopy(src, dst, ssem, rsem, to):
        c = pltpu.make_async_remote_copy(
            src_ref=src, dst_ref=dst, send_sem=ssem, recv_sem=rsem,
            device_id=(to,), device_id_type=pl.DeviceIdType.MESH)
        c.start()

    def got(ref, sem):
        pltpu.make_async_copy(ref, ref, sem).wait()

    def each(fn):
        for p in range(3):
            fn(p)

    def loop(fn):
        def step(p, _):
            fn(p)
            return 0
        lax.fori_loop(0, 3, step, 0)

    own = [pos[0] * wy + pos[1] * wx + pos[2] * wz for wy, wx, wz in ORDER]
    own = [al(16 * (k // 32 * 32 + core * 16 + k % 32)) for k in own]
    cps = []
    for h in range(H):
        for p, w in enumerate((wg_in, wu_in, wd_in)):
            cps.append(pltpu.make_async_copy(
                w.at[:, pl.ds(h * F, F)], wt.at[h * 3 + p, pl.ds(own[p], 16)], loc.at[h * 3 + p]))
    big = [pltpu.make_async_copy(tok_in, tok, loc.at[3 * H]),
           pltpu.make_async_copy(cot_in, og, loc.at[3 * H + 1])]
    for c in cps + big:
        c.start()

    bar = pltpu.get_barrier_semaphore()
    for p in range(3):
        for r in (1, 2, 3):
            pl.semaphore_signal(bar, inc=1, device_id=(dev(p, r),), device_id_type=pl.DeviceIdType.MESH)
    pl.semaphore_signal(bar, inc=1, device_id=(sib,), device_id_type=pl.DeviceIdType.MESH)
    pl.semaphore_wait(bar, 10)
    for c in cps:
        c.wait()

    def base(p):
        sl, mi, fa = ax(p)
        return coord(sl), coord(mi), coord(fa)

    def ag_a(h):
        def fn(p):
            kc, kb, ka = base(p)
            hp = h * 3 + p
            blk = wt.at[hp, pl.ds(al(kc * 512 + core * 256 + kb * 64 + ka * 16), 16)]
            for r in (1, 2, 3):
                rcopy(blk, blk, ss.at[hp], ra.at[hp], dev(ax(p)[2], r))
        each(fn)

    def line(p, hp, kb):
        return wt.at[hp, pl.ds(al(coord(p) * 512 + core * 256 + kb * 64, 64), 64)]

    def send_line(p, hp, kb):
        ref = line(p, hp, kb)
        half = kb // 2
        rcopy(ref, ref, ss.at[hp], rc.at[hp * 4 + half], dev(p, 1))
        rcopy(ref, ref, ss.at[hp], rc.at[hp * 4 + 2 + half], dev(p, 3))

    def ag_b(h):
        def fn(p):
            hp = h * 3 + p
            kb = coord(ax(p)[1])
            got(wt.at[hp, pl.ds(0, 48)], ra.at[hp])
            ref = line(p, hp, kb)
            for r in (1, 2, 3):
                rcopy(ref, ref, ss.at[hp], rb.at[hp], dev(ax(p)[1], r))
            send_line(p, hp, kb)
        each(fn)

    def plane(hp, kc):
        return wt.at[hp, pl.ds(al(kc * 512 + core * 256, 256), 256)]

    def to_sib(p, hp, r):
        ref = plane(hp, (coord(p) + r) % 4)
        rcopy(ref, ref, ss.at[hp], rdg.at[hp * 4 + r], sib)

    def ag_c(h):
        def fn(p):
            hp = h * 3 + p
            kb = coord(ax(p)[1])
            got(wt.at[hp, pl.ds(0, 192)], rb.at[hp])
            for j in (1, 2, 3):
                send_line(p, hp, (kb + j) % 4)
            to_sib(p, hp, 0)
        each(fn)

    def ag_f(h):
        def fn(p):
            hp = h * 3 + p
            low = wt.at[hp, pl.ds(0, 128)]
            got(low, rc.at[hp * 4])
            src = wt.at[hp, pl.ds(al((coord(p) + 3) % 4 * 512 + core * 256, 256), 128)]
            rcopy(src, src, ss.at[hp], rf.at[hp * 2], dev(p, 1))
            got(low, rc.at[hp * 4 + 3])
            src = wt.at[hp, pl.ds(al((coord(p) + 1) % 4 * 512 + core * 256 + 128, 128), 128)]
            rcopy(src, src, ss.at[hp], rf.at[hp * 2 + 1], dev(p, 3))
            got(low, rc.at[hp * 4 + 1])
            to_sib(p, hp, 3)
            got(low, rc.at[hp * 4 + 2])
            to_sib(p, hp, 1)
        each(fn)

    def ag_g(h):
        def fn(p):
            hp = h * 3 + p
            got(wt.at[hp, pl.ds(0, 128)], rf.at[hp * 2])
            got(wt.at[hp, pl.ds(0, 128)], rf.at[hp * 2 + 1])
            to_sib(p, hp, 2)
        each(fn)

    eye = (lax.broadcasted_iota(jnp.int32, (256, 256), 0)
           == lax.broadcasted_iota(jnp.int32, (256, 256), 1)).astype(f32).astype(bf16)

    def turn(src, ps):
        def step(t, _):
            cols = pl.ds(al(t * 256, 256), 256)
            v = lax.dot_general(eye, src[:, cols], NT, preferred_element_type=f32).astype(bf16)
            for p in ps:
                for j in range(16):
                    y, x, z, c = t // 2, t % 2 * 2 + j // 8, j // 2 % 4, j % 2
                    wy, wx, wz = ORDER[p]
                    k = y * wy + x * wx + z * wz
                    row = 16 * (k // 32 * 32 + c * 16 + k % 32)
                    lt[p, pl.ds(al(row), 16), :] = v[j * 16:(j + 1) * 16]
            return 0
        lax.fori_loop(0, 8, step, 0)

    def scale():
        n = tok.shape[0]
        g = gate_in[...].astype(f32)
        g = jnp.where(lax.broadcasted_iota(jnp.int32, (1, n), 1) < count[0], g, 0.0)
        diag = lax.broadcasted_iota(jnp.int32, (n, n), 0) == lax.broadcasted_iota(jnp.int32, (n, n), 1)
        gain[...] = jnp.dot(jnp.where(diag, jnp.broadcast_to(g, (n, n)), 0.0).astype(bf16),
                            jnp.ones((n, 128), bf16), preferred_element_type=f32)

        def step(i, _):
            s = pl.ds(al(i * 32, 32), 32)
            og[s, :] = (gain[s, 0:1] * og[s, :].astype(f32)).astype(bf16)
            return 0
        lax.fori_loop(0, n // 32, step, 0)

    def nat(h, p, ds):
        return jnp.concatenate([wt[h * 3 + p, pl.ds(place(p, d), 16), :] for d in ds], axis=0)

    def nn(h, k):
        for p in ((0, 1), (2,))[k]:
            for r in range(4):
                got(plane(h * 3 + p, r), rdg.at[(h * 3 + p) * 4 + r])
        if k == 0:
            w = jnp.concatenate([nat(h, 0, range(128)), nat(h, 1, range(128))], axis=1)
            v = jnp.dot(tok[...], w, preferred_element_type=f32)
            acc[0] = v[:, :F]
            acc[1] = v[:, F:]
        else:
            acc[2] = jnp.dot(og[...], nat(h, 2, range(128)), preferred_element_type=f32)

    def act(h):
        def step(i, _):
            s = pl.ds(al(i * 64, 64), 64)
            g, u, a = acc[0, s, :], acc[1, s, :], acc[2, s, :]
            sg = jax.nn.sigmoid(g)
            si = g * sg
            gr[h * 3 + 2, s, :] = (si * u).astype(bf16)
            gr[h * 3, s, :] = (a * u * sg * (1.0 + g * (1.0 - sg))).astype(bf16)
            gr[h * 3 + 1, s, :] = (a * si).astype(bf16)
            return 0
        lax.fori_loop(0, 9, step, 0)

    def slot(h, q, r):
        return ((h % 2) * 3 + q) * 4 + r

    def held(h, q, r):
        return part.at[h * 3 + q if r == 0 else 3 * H + (h % 2) * 9 + q * 3 + r - 1]

    def sd_done(h, rs):
        for q in range(3):
            for r in rs:
                got(sd.at[slot(h, q, r)], dS.at[(h * 3 + q) * 4 + r])

    def rs_dot(h, k):
        rs = ((2, 1), (3, 0))[k]
        if h >= 2:
            sd_done(h - 2, rs)

        def fn(q):
            hq = h * 3 + q
            kc = pos[0] + q * (pos[1] - pos[0]) + q * (q - 1) // 2 * (pos[2] - 2 * pos[1] + pos[0])
            rows = []
            for r in rs:
                row = (kc + r) % 4 * 512
                rows.append(lt[q, pl.ds(al(row + 256 - core * 256, 256), 256), :])
                rows.append(lt[q, pl.ds(al(row + core * 256, 256), 256), :])
            v = jnp.dot(jnp.concatenate(rows, axis=0), gr[hq], preferred_element_type=f32)
            for i, r in enumerate(rs):
                at = slot(h, q, r)
                sd[at] = v[i * 512:i * 512 + 256].astype(bf16)
                rcopy(sd.at[at], rd.at[hq * 4 + r], dS.at[hq * 4 + r], dR.at[hq * 4 + r], sib)
                held(h, q, r)[...] = v[i * 512 + 256:(i + 1) * 512]
        loop(fn)

    def rs_far(h):
        def fn(q):
            hq = h * 3 + q
            far = rd.at[hq * 4 + 2]
            got(far, dR.at[hq * 4 + 2])
            far[...] = (held(h, q, 2)[...] + far[...].astype(f32)).astype(bf16)
            lo, hi = pl.ds(0, 128), pl.ds(128, 128)
            rcopy(far.at[lo], cr.at[hq * 3, lo], cS.at[hq * 6], cR.at[hq * 6], dev(q, 1))
            rcopy(far.at[hi], cr.at[hq * 3, hi], cS.at[hq * 6 + 1], cR.at[hq * 6 + 1], dev(q, 3))
        each(fn)

    def rs_near(h, r):
        i, rest = (0, pl.ds(128, 128)) if r == 1 else (1, pl.ds(0, 128))

        def fn(q):
            hq = h * 3 + q
            near = rd.at[hq * 4 + r]
            got(near, dR.at[hq * 4 + r])
            near[rest, :] = (held(h, q, r)[rest, :] + near[rest, :].astype(f32)).astype(bf16)
            rcopy(near.at[rest], cr.at[hq * 3 + 1 + i, rest], cS.at[hq * 6 + 2 + i], cR.at[hq * 6 + 2 + i], dev(q, r))
        each(fn)

    def rs_thru(h, r):
        i, thru = (0, pl.ds(0, 128)) if r == 1 else (1, pl.ds(128, 128))

        def fn(q):
            hq = h * 3 + q
            near = rd.at[hq * 4 + r]
            got(cr.at[hq * 3, thru], cR.at[hq * 6 + i])
            near[thru, :] = (held(h, q, r)[thru, :] + near[thru, :].astype(f32)
                             + cr[hq * 3, thru, :].astype(f32)).astype(bf16)
            rcopy(near.at[thru], cr.at[hq * 3 + 1 + i, thru], cS.at[hq * 6 + 4 + i], cR.at[hq * 6 + 4 + i], dev(q, r))
        each(fn)

    def rs_b(h):
        def fn(q):
            hq = h * 3 + q
            mid = rd.at[hq * 4]
            got(mid, dR.at[hq * 4])
            for i in range(4):
                got(cr.at[hq * 3 + 1, pl.ds(0, 128)], cR.at[hq * 6 + 2 + i])
            v = (held(h, q, 0)[...] + mid[...].astype(f32)
                 + cr[hq * 3 + 1].astype(f32) + cr[hq * 3 + 2].astype(f32))
            held(h, q, 0)[...] = v
            mid[...] = v.astype(bf16)
            b = ax(q)[1]
            kb = coord(b)
            for r in (1, 2, 3):
                rcopy(mid.at[pl.ds(al((kb + r) % 4 * 64, 64), 64)], br.at[hq, pl.ds((r - 1) * 64, 64)],
                      bS.at[hq], bR.at[hq], dev(b, r))
        each(fn)

    def rs_a(h):
        def fn(q):
            hq = h * 3 + q
            _, b, a = ax(q)
            row = al(coord(b) * 64, 64)
            mine = pl.ds(row, 64)
            got(br.at[hq], bR.at[hq])
            v = held(h, q, 0)[mine, :]
            for r in range(3):
                v = v + br[hq, pl.ds(r * 64, 64), :].astype(f32)
            held(h, q, 0)[mine, :] = v
            rd[hq * 4, mine, :] = v.astype(bf16)
            for r in (1, 2, 3):
                rcopy(rd.at[hq * 4, pl.ds(al(row + (coord(a) + r) % 4 * 16), 16)], ar.at[hq, pl.ds((r - 1) * 16, 16)],
                      aS.at[hq], aR.at[hq], dev(a, r))
        each(fn)

    def rs_end(h):
        for q, out in enumerate((out_g, out_u, out_d)):
            hq = h * 3 + q
            _, b, a = ax(q)
            got(ar.at[hq], aR.at[hq])
            v = held(h, q, 0)[pl.ds(al(coord(b) * 64 + coord(a) * 16), 16), :]
            for r in range(3):
                v = v + ar[hq, pl.ds(r * 16, 16), :].astype(f32)
            out[:, h * F:(h + 1) * F] = v

    def rows_out(t):
        ds = range(t * 32, t * 32 + 32)
        cols = pl.ds(t * 512, 512)

        def wide(p):
            return (jnp.concatenate([gr[h * 3 + p] for h in range(H)], axis=1),
                    jnp.concatenate([nat(h, p, ds) for h in range(H)], axis=1))
        mixed[:, cols] = (gain[:, 0:1] * lax.dot_general(*wide(2), NT, preferred_element_type=f32)).astype(bf16)
        tgrad[:, cols] = (lax.dot_general(*wide(0), NT, preferred_element_type=f32)
                          + lax.dot_general(*wide(1), NT, preferred_element_type=f32)).astype(bf16)

    ag_a(0)
    ag_a(1)
    ag_a(2)
    ag_a(3)
    big[0].wait()
    turn(tok, (0, 1))
    ag_b(0)
    big[1].wait()
    scale()
    ag_b(1)
    turn(og, (2,))
    ag_c(0)
    ag_c(1)
    ag_f(0)
    ag_b(2)
    ag_f(1)
    ag_b(3)
    ag_g(0)
    nn(0, 0)
    ag_c(2)
    nn(0, 1)
    act(0)
    rs_dot(0, 0)
    ag_g(1)
    ag_c(3)
    rs_dot(0, 1)
    nn(1, 1)
    ag_f(2)
    rs_near(0, 3)
    rs_near(0, 1)
    nn(1, 0)
    act(1)
    rs_dot(1, 0)
    rs_far(0)
    ag_f(3)
    ag_g(2)
    rs_far(1)
    rs_dot(1, 1)
    nn(2, 0)
    rs_thru(0, 1)
    rs_near(1, 3)
    nn(2, 1)
    rs_near(1, 1)
    ag_g(3)
    act(2)
    rs_thru(0, 3)
    rs_dot(2, 0)
    nn(3, 1)
    rs_far(2)
    rs_near(2, 1)
    rs_thru(1, 3)
    rs_dot(2, 1)
    nn(3, 0)
    rs_near(2, 3)
    rs_thru(1, 1)
    rs_thru(2, 3)
    act(3)
    rs_thru(2, 1)
    rs_dot(3, 0)
    rs_far(3)
    rs_b(0)
    rs_dot(3, 1)
    rs_near(3, 1)
    rs_near(3, 3)
    rs_thru(3, 3)
    rs_thru(3, 1)
    rs_b(1)
    rs_b(2)
    rs_a(0)
    rows_out(0)
    rs_b(3)
    rows_out(1)
    rs_a(1)
    rows_out(2)
    rs_a(2)
    rs_a(3)
    rs_end(1)
    rows_out(3)
    rs_end(2)
    rs_end(0)
    rs_end(3)

    for h in (H - 2, H - 1):
        sd_done(h, range(4))
    for hp in range(3 * H):
        got(wt.at[hp, pl.ds(0, 2032)], ss.at[hp])
        for i in range(6):
            got(rd.at[hp, pl.ds(0, 128)], cS.at[hp * 6 + i])
        got(br.at[hp], bS.at[hp])
        got(ar.at[hp], aS.at[hp])


def deliver(*refs):
    n = len(refs) // 2
    cps = [pltpu.make_async_copy(refs[i], refs[n + i], refs[2 * n].at[i]) for i in range(n)]
    for c in cps:
        c.start()
    for c in cps:
        c.wait()


def body(tokens, route_gate, cotangent, row_count, w_gate, w_up, w_down):
    rows, width = tokens.shape
    ff = w_gate.shape[1]
    F = ff // H
    anyspace = pl.BlockSpec(memory_space=pl.ANY)
    vmem = pl.BlockSpec(memory_space=pltpu.VMEM)
    dma = pltpu.SemaphoreType.DMA
    n = 3 * H
    parts = pl.pallas_call(
        kernel,
        out_shape=(
            pltpu.VMEM((rows, width), bf16),
            pltpu.VMEM((rows, width), bf16),
            pltpu.VMEM((16, ff), f32),
            pltpu.VMEM((16, ff), f32),
            pltpu.VMEM((16, ff), f32),
        ),
        in_specs=[anyspace, anyspace, vmem, pl.BlockSpec(memory_space=pltpu.SMEM), anyspace, anyspace, anyspace],
        out_specs=[vmem] * 5,
        scratch_shapes=[
            pltpu.VMEM((rows, width), bf16),
            pltpu.VMEM((rows, width), bf16),
            pltpu.VMEM((rows, 128), f32),
            pltpu.VMEM((n, width, F), bf16),
            pltpu.VMEM((3, width, rows), bf16),
            pltpu.VMEM((3, rows, F), f32),
            pltpu.VMEM((n, rows, F), bf16),
            pltpu.VMEM((n + 18, 256, F), f32),
            pltpu.VMEM((24, 256, F), bf16),
            pltpu.VMEM((n * 4, 256, F), bf16),
            pltpu.VMEM((n * 3, 256, F), bf16),
            pltpu.VMEM((n, 192, F), bf16),
            pltpu.VMEM((n, 48, F), bf16),
            dma((n + 2,)), dma((n,)), dma((n,)), dma((n,)), dma((n * 4,)), dma((n * 2,)), dma((n * 4,)),
            dma((n * 4,)), dma((n * 4,)), dma((n * 6,)), dma((n * 6,)),
            dma((n,)), dma((n,)), dma((n,)), dma((n,)),
        ],
        compiler_params=pltpu.CompilerParams(
            collective_id=0, has_side_effects=True, vmem_limit_bytes=57 * 1024 * 1024),
        cost_estimate=pl.CostEstimate(
            flops=18 * rows * width * ff, bytes_accessed=8 * rows * width, transcendentals=rows * ff),
    )(tokens, cotangent, route_gate[None, :], row_count, w_gate, w_up, w_down)
    return pl.pallas_call(
        deliver,
        out_shape=tuple(jax.ShapeDtypeStruct(v.shape, v.dtype) for v in parts),
        in_specs=[vmem] * 5,
        out_specs=[anyspace] * 5,
        scratch_shapes=[dma((5,))],
        compiler_params=pltpu.CompilerParams(vmem_limit_bytes=1024 * 1024),
    )(*parts)


def solution(mesh):
    row, vec = P("dp", None), P("dp")
    return jax.shard_map(
        body,
        mesh=mesh,
        in_specs=(row, vec, row, vec, row, row, row),
        out_specs=(row,) * 5,
        check_vma=False,
    )
```

time: 95 us -> 83.2 us (0.88)
  local copies, waits for them, and re-layouts: 7.68 us -> 1.26 us
  Pallas kernels: 85.2 us -> 80.3 us
    unnamed x13 -> x0, local copies, waits for them, and re-layouts: 6.82 us -> none
    pallas_call x1 -> x2, Pallas kernels: 85.2 us -> 80.3 us  [the longest x1 78.1 us: body(): pl.pallas_call(kernel, out_shape=(pltpu.VMEM((rows, width), bf16), pltpu....]
where the time goes in v2:
time: 83.2 us; the launch traced here: 83.1 us
  Pallas kernels  80.3 us (97%)
  between operations  1.45 us (2%)
  local copies, waits for them, and re-layouts  1.26 us (2%)
    pallas_call x1, Pallas kernels, body(): pl.pallas_call(kernel, out_shape=(pltpu.VMEM((rows, width), bf16), pltpu....  78.1 us
    pallas_call x1, Pallas kernels, body(): pl.pallas_call(deliver, out_shape=tuple((jax.ShapeDtypeStruct(v.shape, v....  2.27 us

profile of v2, /device:TPU:0, one launch (start us, length us, event | category | flops | bytes accessed | tf_op | source)
XLA Modules:
  0.0 83.1 jit_solution(12544970231395896503)
XLA Ops:
  1.3 1.3 %broadcast_in_dim.3.gate_in = bf16[1,576]{1,0:T(2,128)(2,1)} reshape(bf16[576]{0:T(1024)(128)(2,1)} %param.8) | data formatting | bytes 2304 | tf_op jit(solution)/shard_map/broadcast_in_dim | solution.py:486
  2.5 78.1 %shard_map.110 = (bf16[576,2048]{1,0:T(8,128)(2,1)S(1)}, bf16[576,2048]{1,0:T(8,128)(2,1)S(1)}, f32[16,1024]{1,0:T(8,128)S(1)}, f32[16,1024]{1,0:T(8,128)S(1)}, f32[16,1024]{1,0:T(8,128)S(1)}) custom-call(bf16[576,2048]{1,0:T(8,128)(2,1)} %tok_in.1, bf16[576,2048]{1,0:T(8,128)(2,1)} %cot_in.1, bf16[1,576]{1,0:T(2,128)(2,1)} %broadcast_in_dim.3.gate_in, ...), custom_call_target="tpu_custom_call" | custom-call | flops 21743271936 | bytes 9437184 | tf_op jit(solution)/shard_map/pallas_call | solution.py:453
  80.6 2.3 %shard_map.111 = (bf16[576,2048]{1,0:T(8,128)(2,1)}, bf16[576,2048]{1,0:T(8,128)(2,1)}, f32[16,1024]{1,0:T(8,128)}, f32[16,1024]{1,0:T(8,128)}, f32[16,1024]{1,0:T(8,128)}) custom-call(bf16[576,2048]{1,0:T(8,128)(2,1)S(1)} %get-tuple-element.10.refs_0_, bf16[576,2048]{1,0:T(8,128)(2,1)S(1)} %get-tuple-element.11.refs_1_, ...), custom_call_target="tpu_custom_call" | custom-call | tf_op jit(solution)/shard_map/pallas_call | solution.py:487

commit v3 on v2

--- a/solution.py
+++ b/solution.py
@@ -11,6 +11,10 @@
 f32 = jnp.float32
 H = 4
 NT = (((1,), (1,)), ((), ()))
+FAR_GATHER = ()
+FAR_REDUCE = ()
+PLANE_GATHER = (0, 1,)
+PLANE_REDUCE = (3,)
 ORDER = ((32, 4, 1), (1, 32, 4), (4, 1, 32))
 
 
@@ -38,6 +42,10 @@
     pos = (me // 32, me // 8 % 4, me // 2 % 4)
     peer = [[me + ((pos[p] + r) % 4 - pos[p]) * st for r in range(4)] for p, st in enumerate((32, 8, 2))]
 
+    def across(p, rb, ra):
+        _, b, a = ax(p)
+        return peer[b][rb] + peer[a][ra] - me
+
     def coord(p):
         return pos[p]
 
@@ -59,12 +67,6 @@
     def each(fn):
         for p in range(3):
             fn(p)
-
-    def loop(fn):
-        def step(p, _):
-            fn(p)
-            return 0
-        lax.fori_loop(0, 3, step, 0)
 
     own = [pos[0] * wy + pos[1] * wx + pos[2] * wz for wy, wx, wz in ORDER]
     own = [al(16 * (k // 32 * 32 + core * 16 + k % 32)) for k in own]
@@ -79,11 +81,12 @@
         c.start()
 
     bar = pltpu.get_barrier_semaphore()
-    for p in range(3):
-        for r in (1, 2, 3):
-            pl.semaphore_signal(bar, inc=1, device_id=(dev(p, r),), device_id_type=pl.DeviceIdType.MESH)
-    pl.semaphore_signal(bar, inc=1, device_id=(sib,), device_id_type=pl.DeviceIdType.MESH)
-    pl.semaphore_wait(bar, 10)
+    meet = [dev(p, r) for p in range(3) for r in (1, 2, 3)] + [sib]
+    if PLANE_GATHER or PLANE_REDUCE:
+        meet += [across(p, rb, ra) for p in range(3) for rb in (1, 2, 3) for ra in (1, 2, 3)]
+    for to in meet:
+        pl.semaphore_signal(bar, inc=1, device_id=(to,), device_id_type=pl.DeviceIdType.MESH)
+    pl.semaphore_wait(bar, len(meet))
     for c in cps:
         c.wait()
 
@@ -96,6 +99,10 @@
             kc, kb, ka = base(p)
             hp = h * 3 + p
             blk = wt.at[hp, pl.ds(al(kc * 512 + core * 256 + kb * 64 + ka * 16), 16)]
+            if h in PLANE_GATHER:
+                for i in range(1, 16):
+                    rcopy(blk, blk, ss.at[hp], rb.at[hp], across(p, i // 4, i % 4))
+                return
             for r in (1, 2, 3):
                 rcopy(blk, blk, ss.at[hp], ra.at[hp], dev(ax(p)[2], r))
         each(fn)
@@ -108,11 +115,15 @@
         half = kb // 2
         rcopy(ref, ref, ss.at[hp], rc.at[hp * 4 + half], dev(p, 1))
         rcopy(ref, ref, ss.at[hp], rc.at[hp * 4 + 2 + half], dev(p, 3))
+        if hp // 3 in FAR_GATHER:
+            rcopy(ref, ref, ss.at[hp], rf.at[hp * 2 + half], dev(p, 2))
 
     def ag_b(h):
         def fn(p):
             hp = h * 3 + p
             kb = coord(ax(p)[1])
+            if h in PLANE_GATHER:
+                return
             got(wt.at[hp, pl.ds(0, 48)], ra.at[hp])
             ref = line(p, hp, kb)
             for r in (1, 2, 3):
@@ -131,8 +142,8 @@
         def fn(p):
             hp = h * 3 + p
             kb = coord(ax(p)[1])
-            got(wt.at[hp, pl.ds(0, 192)], rb.at[hp])
-            for j in (1, 2, 3):
+            got(wt.at[hp, pl.ds(0, 240 if h in PLANE_GATHER else 192)], rb.at[hp])
+            for j in range(0 if h in PLANE_GATHER else 1, 4):
                 send_line(p, hp, (kb + j) % 4)
             to_sib(p, hp, 0)
         each(fn)
@@ -142,11 +153,13 @@
             hp = h * 3 + p
             low = wt.at[hp, pl.ds(0, 128)]
             got(low, rc.at[hp * 4])
-            src = wt.at[hp, pl.ds(al((coord(p) + 3) % 4 * 512 + core * 256, 256), 128)]
-            rcopy(src, src, ss.at[hp], rf.at[hp * 2], dev(p, 1))
+            if h not in FAR_GATHER:
+                src = wt.at[hp, pl.ds(al((coord(p) + 3) % 4 * 512 + core * 256, 256), 128)]
+                rcopy(src, src, ss.at[hp], rf.at[hp * 2], dev(p, 1))
             got(low, rc.at[hp * 4 + 3])
-            src = wt.at[hp, pl.ds(al((coord(p) + 1) % 4 * 512 + core * 256 + 128, 128), 128)]
-            rcopy(src, src, ss.at[hp], rf.at[hp * 2 + 1], dev(p, 3))
+            if h not in FAR_GATHER:
+                src = wt.at[hp, pl.ds(al((coord(p) + 1) % 4 * 512 + core * 256 + 128, 128), 128)]
+                rcopy(src, src, ss.at[hp], rf.at[hp * 2 + 1], dev(p, 3))
             got(low, rc.at[hp * 4 + 1])
             to_sib(p, hp, 3)
             got(low, rc.at[hp * 4 + 2])
@@ -161,13 +174,10 @@
             to_sib(p, hp, 2)
         each(fn)
 
-    eye = (lax.broadcasted_iota(jnp.int32, (256, 256), 0)
-           == lax.broadcasted_iota(jnp.int32, (256, 256), 1)).astype(f32).astype(bf16)
-
     def turn(src, ps):
         def step(t, _):
             cols = pl.ds(al(t * 256, 256), 256)
-            v = lax.dot_general(eye, src[:, cols], NT, preferred_element_type=f32).astype(bf16)
+            v = src[:, cols].T
             for p in ps:
                 for j in range(16):
                     y, x, z, c = t // 2, t % 2 * 2 + j // 8, j // 2 % 4, j % 2
@@ -180,7 +190,7 @@
 
     def scale():
         n = tok.shape[0]
-        g = gate_in[...].astype(f32)
+        g = gate_in[...].astype(f32).reshape(1, n)
         g = jnp.where(lax.broadcasted_iota(jnp.int32, (1, n), 1) < count[0], g, 0.0)
         diag = lax.broadcasted_iota(jnp.int32, (n, n), 0) == lax.broadcasted_iota(jnp.int32, (n, n), 1)
         gain[...] = jnp.dot(jnp.where(diag, jnp.broadcast_to(g, (n, n)), 0.0).astype(bf16),
@@ -235,21 +245,20 @@
         if h >= 2:
             sd_done(h - 2, rs)
 
-        def fn(q):
-            hq = h * 3 + q
-            kc = pos[0] + q * (pos[1] - pos[0]) + q * (q - 1) // 2 * (pos[2] - 2 * pos[1] + pos[0])
+        for q in range(3):
             rows = []
             for r in rs:
-                row = (kc + r) % 4 * 512
+                row = (pos[q] + r) % 4 * 512
                 rows.append(lt[q, pl.ds(al(row + 256 - core * 256, 256), 256), :])
                 rows.append(lt[q, pl.ds(al(row + core * 256, 256), 256), :])
-            v = jnp.dot(jnp.concatenate(rows, axis=0), gr[hq], preferred_element_type=f32)
+            v = jnp.dot(jnp.concatenate(rows, axis=0), gr[h * 3 + q], preferred_element_type=f32)
             for i, r in enumerate(rs):
-                at = slot(h, q, r)
-                sd[at] = v[i * 512:i * 512 + 256].astype(bf16)
-                rcopy(sd.at[at], rd.at[hq * 4 + r], dS.at[hq * 4 + r], dR.at[hq * 4 + r], sib)
+                sd[slot(h, q, r)] = v[i * 512:i * 512 + 256].astype(bf16)
                 held(h, q, r)[...] = v[i * 512 + 256:(i + 1) * 512]
-        loop(fn)
+        for q in range(3):
+            hq = h * 3 + q
+            for r in rs:
+                rcopy(sd.at[slot(h, q, r)], rd.at[hq * 4 + r], dS.at[hq * 4 + r], dR.at[hq * 4 + r], sib)
 
     def rs_far(h):
         def fn(q):
@@ -257,6 +266,9 @@
             far = rd.at[hq * 4 + 2]
             got(far, dR.at[hq * 4 + 2])
             far[...] = (held(h, q, 2)[...] + far[...].astype(f32)).astype(bf16)
+            if h in FAR_REDUCE:
+                rcopy(far, cr.at[hq * 3], cS.at[hq * 6], cR.at[hq * 6], dev(q, 2))
+                return
             lo, hi = pl.ds(0, 128), pl.ds(128, 128)
             rcopy(far.at[lo], cr.at[hq * 3, lo], cS.at[hq * 6], cR.at[hq * 6], dev(q, 1))
             rcopy(far.at[hi], cr.at[hq * 3, hi], cS.at[hq * 6 + 1], cR.at[hq * 6 + 1], dev(q, 3))
@@ -264,6 +276,8 @@
 
     def rs_near(h, r):
         i, rest = (0, pl.ds(128, 128)) if r == 1 else (1, pl.ds(0, 128))
+        if h in FAR_REDUCE:
+            rest = pl.ds(0, 256)
 
         def fn(q):
             hq = h * 3 + q
@@ -275,6 +289,8 @@
 
     def rs_thru(h, r):
         i, thru = (0, pl.ds(0, 128)) if r == 1 else (1, pl.ds(128, 128))
+        if h in FAR_REDUCE:
+            return
 
         def fn(q):
             hq = h * 3 + q
@@ -285,19 +301,37 @@
             rcopy(near.at[thru], cr.at[hq * 3 + 1 + i, thru], cS.at[hq * 6 + 4 + i], cR.at[hq * 6 + 4 + i], dev(q, r))
         each(fn)
 
+    def slow_done(hq, sem, halves, first):
+        whole, half = cr.at[hq * 3 + 1], cr.at[hq * 3 + 1, pl.ds(0, 128)]
+        if halves:
+            for i in range(0 if first else 2, 6):
+                got(half, sem.at[hq * 6 + i])
+        else:
+            for i in (0, 2, 3):
+                got(whole, sem.at[hq * 6 + i])
+
     def rs_b(h):
         def fn(q):
             hq = h * 3 + q
             mid = rd.at[hq * 4]
             got(mid, dR.at[hq * 4])
-            for i in range(4):
-                got(cr.at[hq * 3 + 1, pl.ds(0, 128)], cR.at[hq * 6 + 2 + i])
+            slow_done(hq, cR, h not in FAR_REDUCE, False)
             v = (held(h, q, 0)[...] + mid[...].astype(f32)
                  + cr[hq * 3 + 1].astype(f32) + cr[hq * 3 + 2].astype(f32))
+            if h in FAR_REDUCE:
+                v = v + cr[hq * 3].astype(f32)
             held(h, q, 0)[...] = v
             mid[...] = v.astype(bf16)
-            b = ax(q)[1]
+            _, b, a = ax(q)
             kb = coord(b)
+            if h in PLANE_REDUCE:
+                for i in range(1, 16):
+                    src = mid.at[pl.ds(al((kb + i // 4) % 4 * 64 + (coord(a) + i % 4) % 4 * 16), 16)]
+                    if i < 13:
+                        rcopy(src, br.at[hq, pl.ds(i * 16 - 16, 16)], bS.at[hq], bR.at[hq], across(q, i // 4, i % 4))
+                    else:
+                        rcopy(src, ar.at[hq, pl.ds(i * 16 - 208, 16)], aS.at[hq], aR.at[hq], across(q, i // 4, i % 4))
+                return
             for r in (1, 2, 3):
                 rcopy(mid.at[pl.ds(al((kb + r) % 4 * 64, 64), 64)], br.at[hq, pl.ds((r - 1) * 64, 64)],
                       bS.at[hq], bR.at[hq], dev(b, r))
@@ -309,6 +343,8 @@
             _, b, a = ax(q)
             row = al(coord(b) * 64, 64)
             mine = pl.ds(row, 64)
+            if h in PLANE_REDUCE:
+                return
             got(br.at[hq], bR.at[hq])
             v = held(h, q, 0)[mine, :]
             for r in range(3):
@@ -328,6 +364,10 @@
             v = held(h, q, 0)[pl.ds(al(coord(b) * 64 + coord(a) * 16), 16), :]
             for r in range(3):
                 v = v + ar[hq, pl.ds(r * 16, 16), :].astype(f32)
+            if h in PLANE_REDUCE:
+                got(br.at[hq], bR.at[hq])
+                for r in range(12):
+                    v = v + br[hq, pl.ds(r * 16, 16), :].astype(f32)
             out[:, h * F:(h + 1) * F] = v
 
     def rows_out(t):
@@ -345,80 +385,77 @@
     ag_a(1)
     ag_a(2)
     ag_a(3)
+    big[1].wait()
+    scale()
     big[0].wait()
     turn(tok, (0, 1))
-    ag_b(0)
-    big[1].wait()
-    scale()
-    ag_b(1)
-    turn(og, (2,))
     ag_c(0)
     ag_c(1)
+    turn(og, (2,))
     ag_f(0)
     ag_b(2)
     ag_f(1)
     ag_b(3)
     ag_g(0)
     nn(0, 0)
-    ag_c(2)
     nn(0, 1)
     act(0)
+    ag_c(2)
+    ag_g(1)
+    rs_dot(0, 1)
+    ag_c(3)
+    nn(1, 1)
     rs_dot(0, 0)
-    ag_g(1)
-    ag_c(3)
-    rs_dot(0, 1)
-    nn(1, 1)
     ag_f(2)
-    rs_near(0, 3)
-    rs_near(0, 1)
     nn(1, 0)
     act(1)
+    ag_f(3)
     rs_dot(1, 0)
     rs_far(0)
-    ag_f(3)
     ag_g(2)
+    rs_near(0, 1)
+    rs_dot(1, 1)
+    rs_near(0, 3)
     rs_far(1)
-    rs_dot(1, 1)
-    nn(2, 0)
-    rs_thru(0, 1)
-    rs_near(1, 3)
     nn(2, 1)
     rs_near(1, 1)
+    nn(2, 0)
+    act(2)
+    rs_near(1, 3)
     ag_g(3)
-    act(2)
     rs_thru(0, 3)
+    rs_thru(0, 1)
     rs_dot(2, 0)
+    nn(3, 0)
+    rs_far(2)
+    rs_dot(2, 1)
+    rs_thru(1, 3)
+    rs_thru(1, 1)
     nn(3, 1)
-    rs_far(2)
+    act(3)
     rs_near(2, 1)
-    rs_thru(1, 3)
-    rs_dot(2, 1)
-    nn(3, 0)
     rs_near(2, 3)
-    rs_thru(1, 1)
+    rs_dot(3, 0)
     rs_thru(2, 3)
-    act(3)
     rs_thru(2, 1)
-    rs_dot(3, 0)
+    rs_dot(3, 1)
     rs_far(3)
+    rs_near(3, 1)
+    rs_b(1)
+    rs_near(3, 3)
+    rows_out(0)
+    rs_thru(3, 1)
+    rs_thru(3, 3)
+    rs_b(2)
     rs_b(0)
-    rs_dot(3, 1)
-    rs_near(3, 1)
-    rs_near(3, 3)
-    rs_thru(3, 3)
-    rs_thru(3, 1)
-    rs_b(1)
-    rs_b(2)
+    rows_out(1)
+    rs_b(3)
+    rows_out(2)
     rs_a(0)
-    rows_out(0)
-    rs_b(3)
-    rows_out(1)
     rs_a(1)
-    rows_out(2)
     rs_a(2)
-    rs_a(3)
+    rows_out(3)
     rs_end(1)
-    rows_out(3)
     rs_end(2)
     rs_end(0)
     rs_end(3)
@@ -427,8 +464,7 @@
         sd_done(h, range(4))
     for hp in range(3 * H):
         got(wt.at[hp, pl.ds(0, 2032)], ss.at[hp])
-        for i in range(6):
-            got(rd.at[hp, pl.ds(0, 128)], cS.at[hp * 6 + i])
+        slow_done(hp, cS, hp // 3 not in FAR_REDUCE, True)
         got(br.at[hp], bS.at[hp])
         got(ar.at[hp], aS.at[hp])
 
@@ -483,7 +519,7 @@
             collective_id=0, has_side_effects=True, vmem_limit_bytes=57 * 1024 * 1024),
         cost_estimate=pl.CostEstimate(
             flops=18 * rows * width * ff, bytes_accessed=8 * rows * width, transcendentals=rows * ff),
-    )(tokens, cotangent, route_gate[None, :], row_count, w_gate, w_up, w_down)
+    )(tokens, cotangent, route_gate, row_count, w_gate, w_up, w_down)
     return pl.pallas_call(
         deliver,
         out_shape=tuple(jax.ShapeDtypeStruct(v.shape, v.dtype) for v in parts),

time: 83.2 us -> 81 us (0.974)
  local copies, waits for them, and re-layouts: 1.26 us -> 0 us
    broadcast_in_dim x1 -> x0, local copies, waits for them, and re-layouts: 1.26 us -> none  [body(): route_gate[None, :]]
    pallas_call x1, Pallas kernels: 78.1 us -> 77.2 us  [body(): pl.pallas_call(kernel, out_shape=(pltpu.VMEM((rows, width), bf16), pltpu....]
where the time goes in v3:
time: 81 us; the launch traced here: 80.9 us
  Pallas kernels  79.5 us (98%)
  between operations  1.45 us (2%)
    pallas_call x1, Pallas kernels, body(): pl.pallas_call(kernel, out_shape=(pltpu.VMEM((rows, width), bf16), pltpu....  77.2 us
    pallas_call x1, Pallas kernels, body(): pl.pallas_call(deliver, out_shape=tuple((jax.ShapeDtypeStruct(v.shape, v....  2.27 us

profile of v3, /device:TPU:0, one launch (start us, length us, event | category | flops | bytes accessed | tf_op | source)
XLA Modules:
  0.0 80.9 jit_solution(7136298818163257204)
XLA Ops:
  1.3 77.2 %shard_map.110 = (bf16[576,2048]{1,0:T(8,128)(2,1)S(1)}, bf16[576,2048]{1,0:T(8,128)(2,1)S(1)}, f32[16,1024]{1,0:T(8,128)S(1)}, f32[16,1024]{1,0:T(8,128)S(1)}, f32[16,1024]{1,0:T(8,128)S(1)}) custom-call(bf16[576,2048]{1,0:T(8,128)(2,1)} %tok_in.1, bf16[576,2048]{1,0:T(8,128)(2,1)} %cot_in.1, bf16[576]{0:T(1024)(128)(2,1)} %gate_in.1, s32[1]{0:T(128)S(6)} %copy.12.count, ...), custom_call_target="tpu_custom_call" | custom-call | flops 21743271936 | bytes 9437184 | tf_op jit(solution)/shard_map/pallas_call | solution.py:489
  78.5 2.3 %shard_map.111 = (bf16[576,2048]{1,0:T(8,128)(2,1)}, bf16[576,2048]{1,0:T(8,128)(2,1)}, f32[16,1024]{1,0:T(8,128)}, f32[16,1024]{1,0:T(8,128)}, f32[16,1024]{1,0:T(8,128)}) custom-call(bf16[576,2048]{1,0:T(8,128)(2,1)S(1)} %get-tuple-element.10.refs_0_, bf16[576,2048]{1,0:T(8,128)(2,1)S(1)} %get-tuple-element.11.refs_1_, ...), custom_call_target="tpu_custom_call" | custom-call | tf_op jit(solution)/shard_map/pallas_call | solution.py:523

commit v4 on v3

--- a/solution.py
+++ b/solution.py
@@ -389,9 +389,9 @@
     scale()
     big[0].wait()
     turn(tok, (0, 1))
+    turn(og, (2,))
     ag_c(0)
     ag_c(1)
-    turn(og, (2,))
     ag_f(0)
     ag_b(2)
     ag_f(1)
@@ -402,39 +402,40 @@
     act(0)
     ag_c(2)
     ag_g(1)
+    rs_dot(0, 0)
+    nn(1, 0)
+    rs_far(0)
+    nn(1, 1)
+    act(1)
+    ag_f(2)
     rs_dot(0, 1)
     ag_c(3)
-    nn(1, 1)
-    rs_dot(0, 0)
-    ag_f(2)
-    nn(1, 0)
-    act(1)
+    rs_dot(1, 1)
+    rs_near(0, 1)
+    rs_thru(0, 1)
+    rs_near(0, 3)
+    rs_thru(0, 3)
+    ag_g(2)
+    rs_dot(1, 0)
+    nn(2, 1)
     ag_f(3)
-    rs_dot(1, 0)
-    rs_far(0)
-    ag_g(2)
-    rs_near(0, 1)
-    rs_dot(1, 1)
-    rs_near(0, 3)
+    nn(2, 0)
     rs_far(1)
-    nn(2, 1)
-    rs_near(1, 1)
-    nn(2, 0)
     act(2)
     rs_near(1, 3)
+    rs_dot(2, 0)
+    rs_near(1, 1)
     ag_g(3)
-    rs_thru(0, 3)
-    rs_thru(0, 1)
-    rs_dot(2, 0)
-    nn(3, 0)
+    rs_dot(2, 1)
     rs_far(2)
-    rs_dot(2, 1)
-    rs_thru(1, 3)
+    rs_b(0)
     rs_thru(1, 1)
     nn(3, 1)
+    rs_near(2, 3)
+    rs_thru(1, 3)
+    rs_near(2, 1)
+    nn(3, 0)
     act(3)
-    rs_near(2, 1)
-    rs_near(2, 3)
     rs_dot(3, 0)
     rs_thru(2, 3)
     rs_thru(2, 1)
@@ -447,17 +448,16 @@
     rs_thru(3, 1)
     rs_thru(3, 3)
     rs_b(2)
-    rs_b(0)
     rows_out(1)
+    rs_a(0)
+    rs_a(1)
     rs_b(3)
     rows_out(2)
-    rs_a(0)
-    rs_a(1)
     rs_a(2)
     rows_out(3)
     rs_end(1)
+    rs_end(0)
     rs_end(2)
-    rs_end(0)
     rs_end(3)
 
     for h in (H - 2, H - 1):

time: 81 us -> 81.1 us (level)
  no operation moved by 1% of the time
where the time goes in v4:
time: 81.1 us; the launch traced here: 81 us
  Pallas kernels  79.5 us (98%)
  between operations  1.45 us (2%)
    pallas_call x1, Pallas kernels, body(): pl.pallas_call(kernel, out_shape=(pltpu.VMEM((rows, width), bf16), pltpu....  77.2 us
    pallas_call x1, Pallas kernels, body(): pl.pallas_call(deliver, out_shape=tuple((jax.ShapeDtypeStruct(v.shape, v....  2.27 us

profile of v4, /device:TPU:0, one launch (start us, length us, event | category | flops | bytes accessed | tf_op | source)
XLA Modules:
  0.0 81.0 jit_solution(3043580980857726173)
XLA Ops:
  1.3 77.2 %shard_map.110 = (bf16[576,2048]{1,0:T(8,128)(2,1)S(1)}, bf16[576,2048]{1,0:T(8,128)(2,1)S(1)}, f32[16,1024]{1,0:T(8,128)S(1)}, f32[16,1024]{1,0:T(8,128)S(1)}, f32[16,1024]{1,0:T(8,128)S(1)}) custom-call(bf16[576,2048]{1,0:T(8,128)(2,1)} %tok_in.1, bf16[576,2048]{1,0:T(8,128)(2,1)} %cot_in.1, bf16[576]{0:T(1024)(128)(2,1)} %gate_in.1, s32[1]{0:T(128)S(6)} %copy.12.count, ...), custom_call_target="tpu_custom_call" | custom-call | flops 21743271936 | bytes 9437184 | tf_op jit(solution)/shard_map/pallas_call | solution.py:489
  78.5 2.3 %shard_map.111 = (bf16[576,2048]{1,0:T(8,128)(2,1)}, bf16[576,2048]{1,0:T(8,128)(2,1)}, f32[16,1024]{1,0:T(8,128)}, f32[16,1024]{1,0:T(8,128)}, f32[16,1024]{1,0:T(8,128)}) custom-call(bf16[576,2048]{1,0:T(8,128)(2,1)S(1)} %get-tuple-element.10.refs_0_, bf16[576,2048]{1,0:T(8,128)(2,1)S(1)} %get-tuple-element.11.refs_1_, ...), custom_call_target="tpu_custom_call" | custom-call | tf_op jit(solution)/shard_map/pallas_call | solution.py:523
